TPU v7x, 512 devices: a whole 4x8x8 slice. The times are simulated.
512 devices in a mesh: basis: 32 (over z_hi, x, core), aux: 16 (over z_lo, y).
Axes of the slice: x: 4, y: 8, z: 8 (z_hi: 4, z_lo: 2; z = z_hi * 2 + z_lo), core: 2. Of those that a mesh axis runs over, the one named last changes fastest.
Arguments:
- half_three: bfloat16 [16384, 64, 256], P('basis', 'aux'), may hold values from -1.25 to 1.25
- block_mask: int32 [128, 16, 2], P('basis', 'aux'), may hold values 0 or 1
- panel_blocks: int32 [16], replicated, may hold values from 0 to 127, as said below
Outputs:
- exchange_panel: float32 [2048, 16384], P('aux', 'basis')
Inputs may be any that keep to these rules, and one draw needn't show every extreme that they name: `panel_blocks`: distinct basis block numbers; no two lie in the same run of 4 blocks, so each device along basis holds at most one, and exactly 16 devices hold one.
All inputs are finite; a program needn't handle non-finite values. No bound on the sum of `block_mask` on one device may be relied on, other than what follows from the above.
Results may differ from a plain program's by a relative error of at most 0.0003.
Values may be sent and summed in bfloat16 or wider, within the bound.
A program may use at most 64 MiB of HBM per device.

v0:
```python
import jax
import jax.numpy as jnp
from jax import lax
from jax.sharding import PartitionSpec as P


def body(half_three, block_mask, panel_blocks):
    cols, auxw, occ = half_three.shape
    nbb, single, nob = block_mask.shape
    blk = cols // nbb
    width = auxw * occ
    shaped = half_three.reshape(nbb, blk, auxw, nob, blk)
    keep = block_mask[:, None, :, :, None].astype(jnp.bfloat16)
    kept = (shaped * keep).reshape(cols, width)
    rank = lax.axis_index("basis")
    holder = panel_blocks // nbb
    mine = holder == rank
    within = (panel_blocks % nbb)[:, None] == jnp.arange(nbb)[None, :]
    picked = jnp.sum(jnp.logical_and(within, mine[:, None]).astype(jnp.float32), axis=0).astype(
        jnp.bfloat16
    )
    slot = jnp.dot(
        picked[None, :], kept.reshape(nbb, blk * width), preferred_element_type=jnp.float32
    )
    slot = slot.reshape(blk, width).astype(jnp.bfloat16)
    npb = panel_blocks.shape[0]
    every = lax.dot_general(
        lax.all_gather(slot, "basis", axis=0, tiled=True),
        kept,
        (((1,), (1,)), ((), ())),
        preferred_element_type=jnp.float32,
    )
    partial_value = jnp.take(every.reshape(-1, blk, cols), holder, axis=0).reshape(npb * blk, cols)
    return lax.psum_scatter(partial_value, "aux", scatter_dimension=0, tiled=True)


def solution(mesh):
    placed = (P("basis", "aux", None), P("basis", "aux", None), P())
    return jax.shard_map(
        body, mesh=mesh, in_specs=placed, out_specs=P("aux", "basis"), check_vma=False
    )
```

profile of v0, /device:TPU:4, one launch (start us, length us, event | category | flops | bytes accessed | tf_op | source)
XLA Modules:
  0.0 211.4 jit_solution(1163392470947968877)
XLA Ops:
  6.5 0.0 all-gather.2.cloned.1.call-start
  6.5 0.7 compare_and_fusion
  7.2 0.7 and_select_fusion
  7.9 0.7 convert_bitcast_fusion
  8.6 0.1 copy.6
  8.7 0.6 mul.23
  9.3 0.4 mul.24
  9.7 0.0 copy-start
  9.7 1.7 reshape.37
  11.4 0.1 convert_reduce_fusion
  11.5 0.5 mul.25
  12.1 0.7 fusion.1
  12.8 0.8 copy.13
  13.6 0.0 all-gather.2.cloned.1.call-update
  13.6 0.0 reduce-scatter.2.cloned.1.call-start
  13.6 0.2 mul.26
  13.9 0.0 copy-done
  13.9 0.6 broadcast_multiply_fusion
  14.5 0.8 reshape.49
  15.3 0.1 broadcast_bitcast_fusion
  15.4 88.3 %all-gather.2.cloned.1.call-done = bf16[4096,1024]{1,0:T(8,128)(2,1)} async-done(((bf16[128,1024]{1,0:T(8,128)(2,1)}), bf16[4096,1024]{1,0:T(8,128)(2,1)}) %all-gather.2.cloned.1.call-update) | async-done | bytes 8388624 | tf_op jit(solution)/shard_map/all_gather | solution.py:28
  103.7 10.3 %fusion.2 = f32[32,128,512]{2,1,0:T(8,128)} fusion(bf16[32,128,1024]{2,1,0:T(8,128)(2,1)} %bitcast.28, bf16[512,1024,1]{1,0,2:T(8,128)(2,1)S(1)} %reshape.49), kind=kOutput, calls=%fused_computation.21 | convolution fusion | flops 4294967296 | bytes 17825792 | tf_op jit(solution)/shard_map/dot_general | solution.py:27
  114.0 6.1 %gather_fusion = f32[16,128,512]{2,1,0:T(8,128)} fusion(f32[32,128,512]{2,1,0:T(8,128)} %fusion.2, s32[1024]{0:T(1024)S(1)} %pad_clamp_fusion), kind=kCustom, calls=%fused_computation | custom fusion | bytes 8388672 | tf_op jit(solution)/shard_map/jit(_take)/gather | solution.py:33
  120.1 3.8 %bitcast_select_fusion = f32[2048,512]{1,0:T(8,128)} fusion(f32[16,128,512]{2,1,0:T(8,128)} %gather_fusion, pred[2048]{0:T(1024)(128)(4,1)S(1)} %broadcast_bitcast_fusion), kind=kLoop, calls=%fused_computation.1 | loop fusion | flops 1048576 | bytes 8390656 | tf_op jit(solution)/shard_map/jit(_take)/select_n | solution.py:33
  123.9 0.0 reduce-scatter.2.cloned.1.call-update
  123.9 80.7 %reduce-scatter.2.cloned.1.call-done = f32[128,512]{1,0:T(8,128)} async-done(((f32[2048,512]{1,0:T(8,128)}), f32[128,512]{1,0:T(8,128)}) %reduce-scatter.2.cloned.1.call-update) | async-done | bytes 262160 | tf_op jit(solution)/shard_map/reduce_scatter | solution.py:34
  (4 shorter events, 0.1 us)
Async XLA Ops:
  6.5 97.2 %all-gather.2.cloned.1.call-start = ((), (), s32[]{:S(2)}) async-start(), calls=%async_computation.1 | async-start | bytes 8650752 | tf_op jit(solution)/shard_map/all_gather | solution.py:28
  9.7 4.2 %copy-start = (bf16[512,4,256]{2,1,0:T(4,128)(2,1)S(1)}, bf16[512,4,256]{2,1,0:T(4,128)(2,1)}, u32[]{:S(2)}) copy-start(bf16[512,4,256]{2,1,0:T(4,128)(2,1)} %param.3) | copy-start | bytes 3145732
  13.6 191.0 %reduce-scatter.2.cloned.1.call-start = ((), (), s32[]{:S(2)}) async-start(), calls=%async_computation.2 | async-start | bytes 4456448 | tf_op jit(solution)/shard_map/reduce_scatter | solution.py:34
Sparse Core Ops, SparseCore 0:
  13.7 89.9 all-gather.1
  124.0 80.5 reduce-scatter.1
where the time goes:
time: 212 us; the launch traced here: 211 us
  waiting for transfers between devices  169 us (80%)
  between operations  13.5 us (6%)
  matrix products  10.9 us (5%)
  local copies, waits for them, and re-layouts  10.8 us (5%)
  other arithmetic  7.07 us (3%)
    all_gather x1, waiting for transfers between devices, body(): lax.all_gather(slot, 'basis', axis=0, tiled=True)  88.3 us
    reduce_scatter x1, waiting for transfers between devices, body(): lax.psum_scatter(partial_value, 'aux', scatter_dimension=0, tiled=True)  80.7 us
    dot_general x1, matrix products, body(): lax.dot_general(lax.all_gather(slot, 'basis', axis=0, tiled=True), kept,...  10.3 us
    gather x1, local copies, waits for them, and re-layouts, body(): jnp.take(every.reshape(-1, blk, cols), holder, axis=0)  6.15 us
  transfers between devices with their start and end apart: 2, of which 2 were waited for; matrix products, arithmetic and copies ran while one was open for 1% of the time, Pallas kernels for 0%

commit v1 on v0

v1 whole, which is shorter than its diff:
```python
import functools

import jax
import jax.numpy as jnp
from jax import lax
from jax.experimental import pallas as pl
from jax.experimental.pallas import tpu as pltpu
from jax.sharding import PartitionSpec as P

MESH = pl.DeviceIdType.MESH
NZH, NX, NCORE, NZL, NY = 4, 4, 2, 2, 8
NPB = 16
BLK = 128
K8 = 8
CHUNKS = 4
LANES = 4
TOP = 32767.0
LEVELS = 64.0
STAGE_AT = {"across": 0, "compact": 6, "share": 11, "multiply": 13, "hop1": 17, "hop2": 21, "hop3": 25, "merge": 29, "finish": 33}
SPACING = 20.0 / CHUNKS


def rank(zh, x, c):
    return (zh * NX + x) * NCORE + c


def wait_bytes(view, sem):
    pltpu.make_async_copy(view, view, sem).wait()


def encode(values, rows, scales, message):
    for i, value in enumerate(values):
        scales[pl.ds(i, 1), :] = jnp.max(jnp.abs(value), axis=0, keepdims=True)
    most = jnp.maximum(scales[...], 1e-33)
    level = jnp.floor(jnp.log(most) * (LEVELS / 0.6931471805599453)) + 2.0
    factor = jnp.exp(level * (-0.6931471805599453 / LEVELS)) * TOP
    for i, value in enumerate(values):
        message[pl.ds(i * rows, rows), :] = jnp.round(value * factor[i : i + 1, :]).astype(jnp.int32).astype(jnp.int16)
    both = jnp.concatenate([level, jnp.zeros_like(level)], axis=0)
    message[pl.ds(8 * rows, 16), :] = both.astype(jnp.int32).astype(jnp.int16)


def decode(message, rows, count):
    level = message[pl.ds(8 * rows, 16), :].astype(jnp.int32).astype(jnp.float32)
    factor = jnp.exp(level * (0.6931471805599453 / LEVELS)) * (1.0 / TOP)
    return [
        message[pl.ds(i * rows, rows), :].astype(jnp.int32).astype(jnp.float32) * factor[i : i + 1, :]
        for i in range(count)
    ]


def kernel(
    kept, slot, holders, out, panel, part, sent, got, fsent, fgot, own, scales,
    s1s, s1r, s2s, s2r, s3s, s3r, s4s, s4r, rss, rsr, fs, fr, *stage,
):
    rows = BLK // CHUNKS
    b, a = lax.axis_index("basis"), lax.axis_index("aux")
    zh, x, c = b // (NX * NCORE), (b // NCORE) % NX, b % NCORE
    zl, y = a // NY, a % NY
    left, right = (y + NY - 1) % NY, (y + 1) % NY

    def at(zh_, x_, c_):
        return (rank(zh_, x_, c_), a)

    def up(y_, zl_=zl):
        return (b, zl_ * NY + y_)

    row_mates = [(dx, dc) for dx in range(NX) for dc in range(NCORE) if dx or dc]
    barrier = pltpu.get_barrier_semaphore()
    mates = [at(zh, (x + dx) % NX, (c + dc) % NCORE) for dx, dc in row_mates]
    mates += [at((zh + d) % NZH, x, c) for d in range(1, NZH)]
    mates += [up(left), up(right), up(y, 1 - zl)]
    for mate in mates:
        pl.semaphore_signal(barrier, inc=1, device_id=mate, device_id_type=MESH)

    pl.semaphore_wait(barrier, len(mates))

    def remote(src, dst, send, recv, mate):
        pltpu.make_async_remote_copy(
            src_ref=src, dst_ref=dst, send_sem=send, recv_sem=recv, device_id=mate, device_id_type=MESH
        ).start()

    for t in range(CHUNKS):
        piece = pl.ds(t * rows, rows)
        for dx, dc in row_mates:
            x_, c_ = (x + dx) % NX, (c + dc) % NCORE
            remote(
                slot.at[piece, pl.ds(pl.multiple_of((4 * c_ + x_) * 128, 128), 128)], stage[t].at[b], s1s.at[t], s1r.at[t], at(zh, x_, c_)
            )
        stage[t][b] = slot[piece, pl.ds(pl.multiple_of((4 * c + x) * 128, 128), 128)]

    def across(t):
        wait_bytes(stage[t].at[pl.ds(0, 7)], s1r.at[t])
        mine = stage[t].at[pl.ds(zh * 8, 8)]
        for d in (1, 3, 2):
            remote(mine, mine, s2s.at[t], s2r.at[t], at((zh + d) % NZH, x, c))

    eighth = 4 * c + x

    def compact(t):
        wait_bytes(stage[t].at[pl.ds(0, 24)], s2r.at[t])
        for j in range(NPB):
            panel[t, eighth, pl.ds(j * rows, rows), :] = stage[t][holders[j]]
        mine = panel.at[t, eighth]
        for d in (1, 3, 2):
            remote(mine, mine, s3s.at[t], s3r.at[t, d - 1], at(zh, (x + d) % NX, c))
        remote(mine, mine, s3s.at[t], s4r.at[t], at(zh, x, 1 - c))

    def share(t):
        for d in (1, 3, 2):
            came = panel.at[t, 4 * c + (x + NX - d) % NX]
            wait_bytes(came, s3r.at[t, d - 1])
            remote(came, came, s4s.at[t], s4r.at[t], at(zh, x, 1 - c))

    def mine_of(t, dest, half):
        return [part[t, g, dest + NY * half] for g in range(LANES)]

    def multiply(t):
        wait_bytes(panel.at[t, pl.ds(0, 4)], s4r.at[t])
        lhs = jnp.concatenate([panel[t, k] for k in range(K8)], axis=1)
        value = lax.dot_general(lhs, kept[...], (((1,), (1,)), ((), ())), preferred_element_type=jnp.float32)
        for g in range(LANES):
            part[t, g] = value[:, g * 128 : (g + 1) * 128].reshape(NPB, rows, 128)
        dest = (y + 4) % NY
        hop_send(t, 0, 0, mine_of(t, dest, 0) * 2)
        hop_send(t, 1, 0, mine_of(t, dest, 1) * 2)

    def hop_send(t, way, step, values):
        count = 4 if step == 0 else 8
        message = sent.at[t, way, step]
        encode(values, rows, scales, message)
        mate = up(right if way == 0 else left)
        remote(message, got.at[t, way, step], rss.at[t, way, step], rsr.at[t, way, step], mate)

    def received(t, way, step):
        wait_bytes(got.at[t, way, step], rsr.at[t, way, step])
        return decode(got.at[t, way, step], rows, 8)

    def hop(t, step):
        for way in range(2):
            dest = (y + 4 - step) % NY if way == 0 else (y + 4 + step) % NY
            came = received(t, way, step - 1)
            half0, half1 = mine_of(t, dest, 0), mine_of(t, dest, 1)
            if step > 1 or way == 0:
                half0 = [p + q for p, q in zip(half0, came[:4])]
            if step > 1 or way == 1:
                half1 = [p + q for p, q in zip(half1, came[4:])]
            hop_send(t, way, step, half0 + half1)

    def merge(t):
        from_left = received(t, 0, 3)
        from_right = received(t, 1, 3)
        for g in range(LANES):
            for half in range(2):
                i = half * 4 + g
                total = part[t, g, y + NY * half] + (from_left[i] + from_right[i])
                own[half, t, g] = total
        fsent[t] = own[1 - zl, t]
        remote(fsent.at[t], fgot.at[t], fs.at[t], fr.at[t], up(y, 1 - zl))

    def finish(t):
        wait_bytes(fgot.at[t], fr.at[t])
        for g in range(LANES):
            out[pl.ds(t * rows, rows), pl.ds(g * 128, 128)] = own[zl, t, g] + fgot[t, g]

    work = {
        "across": across, "compact": compact, "share": share, "multiply": multiply,
        "hop1": lambda t: hop(t, 1), "hop2": lambda t: hop(t, 2), "hop3": lambda t: hop(t, 3),
        "merge": merge, "finish": finish,
    }
    order = sorted((STAGE_AT[s] + SPACING * t, i, t) for i, s in enumerate(work) for t in range(CHUNKS))
    names = list(work)
    for _, i, t in order:
        work[names[i]](t)

    for t in range(CHUNKS):
        wait_bytes(stage[t].at[pl.ds(0, 7)], s1s.at[t])
        wait_bytes(stage[t].at[pl.ds(0, 24)], s2s.at[t])
        wait_bytes(panel.at[t, pl.ds(0, 4)], s3s.at[t])
        wait_bytes(panel.at[t, pl.ds(0, 3)], s4s.at[t])
        for way in range(2):
            for step in range(4):
                wait_bytes(sent.at[t, way, step], rss.at[t, way, step])
        wait_bytes(fsent.at[t], fs.at[t])


def body(half_three, block_mask, panel_blocks):
    cols, auxw, occ = half_three.shape
    nbb, single, nob = block_mask.shape
    width = auxw * occ
    shaped = half_three.reshape(nbb, BLK, auxw, nob, BLK)
    keep = block_mask[:, None, :, :, None].astype(jnp.bfloat16)
    kept = (shaped * keep).reshape(cols, width)
    holders = panel_blocks // nbb
    mine = holders == lax.axis_index("basis")
    within = jnp.sum(jnp.where(mine, panel_blocks % nbb, 0))
    slot = lax.dynamic_slice(kept, (within * BLK, 0), (BLK, width))
    rows = BLK // CHUNKS
    dma = pltpu.SemaphoreType.DMA
    vmem = pltpu.VMEM
    return pl.pallas_call(
        kernel,
        out_shape=jax.ShapeDtypeStruct((BLK, cols), jnp.float32),
        in_specs=[pl.BlockSpec(memory_space=pltpu.VMEM)] * 2 + [pl.BlockSpec(memory_space=pltpu.SMEM)],
        out_specs=pl.BlockSpec(memory_space=pltpu.VMEM),
        scratch_shapes=[
            vmem((CHUNKS, K8, NPB * rows, 128), jnp.bfloat16),
            vmem((CHUNKS, LANES, NPB, rows, 128), jnp.float32),
            vmem((CHUNKS, 2, 4, 8 * rows + 16, 128), jnp.int16),
            vmem((CHUNKS, 2, 4, 8 * rows + 16, 128), jnp.int16),
            vmem((CHUNKS, LANES, rows, 128), jnp.float32),
            vmem((CHUNKS, LANES, rows, 128), jnp.float32),
            vmem((2, CHUNKS, LANES, rows, 128), jnp.float32),
            vmem((8, 128), jnp.float32),
            dma((CHUNKS,)), dma((CHUNKS,)), dma((CHUNKS,)), dma((CHUNKS,)),
            dma((CHUNKS,)), dma((CHUNKS, 3)), dma((CHUNKS,)), dma((CHUNKS,)),
            dma((CHUNKS, 2, 4)), dma((CHUNKS, 2, 4)), dma((CHUNKS,)), dma((CHUNKS,)),
            *[vmem((32, rows, 128), jnp.bfloat16) for _ in range(CHUNKS)],
        ],
        compiler_params=pltpu.CompilerParams(
            collective_id=0, has_side_effects=True, vmem_limit_bytes=56 << 20
        ),
        cost_estimate=pl.CostEstimate(flops=2 * 2048 * cols * width, bytes_accessed=2 << 20, transcendentals=0),
    )(kept, slot, holders)


def solution(mesh):
    placed = (P("basis", "aux", None), P("basis", "aux", None), P())
    return jax.shard_map(
        body, mesh=mesh, in_specs=placed, out_specs=P("aux", "basis"), check_vma=False
    )
```

time: 212 us -> 93.7 us (0.44)
  the two profiles are of different devices: /device:TPU:4 before, /device:TPU:16 now
where the time goes in v1:
time: 93.7 us; the launch traced here: 93.5 us
  Pallas kernels  85.1 us (91%)
  local copies, waits for them, and re-layouts  6.12 us (7%)
  other arithmetic  1.56 us (2%)
    pallas_call x1, Pallas kernels, body(): pl.pallas_call(kernel, out_shape=jax.ShapeDtypeStruct((BLK, cols), jnp.fl...  85.1 us
    unnamed x10, local copies, waits for them, and re-layouts  3.85 us

profile of v1, /device:TPU:16, one launch (start us, length us, event | category | flops | bytes accessed | tf_op | source)
XLA Modules:
  0.0 93.5 jit_solution(5881262478824571364)
XLA Ops:
  0.0 0.0 copy-start.3
  0.0 0.7 copy-done.3
  0.7 0.0 copy-start.2
  0.7 0.1 copy.4
  0.8 0.5 copy-done.2
  1.3 1.2 %fusion = (s32[]{:T(128)}, s32[16]{0:T(128)}) fusion(s32[]{:T(128)S(6)} %axis_index.15, s32[16]{0:T(128)S(1)} %copy-done.2), kind=kLoop, calls=%fused_computation.7 | loop fusion | flops 351 | bytes 136 | tf_op jit(solution)/shard_map/reduce_sum | solution.py:196
  3.2 0.6 mul.14
  3.8 0.0 copy-start.1
  3.8 0.8 mul.15
  4.5 0.4 copy-done.1
  5.0 0.2 copy.5
  5.2 0.4 mul.16.kept
  5.6 0.0 copy-start
  5.6 0.8 constant_dynamic-slice_fusion.slot
  6.4 0.3 copy-done
  6.7 85.1 %shard_map.37 = f32[128,512]{1,0:T(8,128)} custom-call(bf16[512,1024]{1,0:T(8,128)(2,1)} %copy-done, bf16[128,1024]{1,0:T(8,128)(2,1)} %constant_dynamic-slice_fusion.slot, s32[16]{0:T(128)} %get-tuple-element.6.holders), custom_call_target="tpu_custom_call" | custom-call | flops 2147483648 | bytes 2097152 | tf_op jit(solution)/shard_map/pallas_call | solution.py:201
  91.8 1.7 %copy.7 = f32[128,512]{1,0:T(8,128)} copy(f32[128,512]{1,0:T(8,128)} %shard_map.37) | data formatting | bytes 524288
  (1 shorter events, 0.0 us)
Async XLA Ops:
  0.0 0.7 copy-start.3
  0.7 0.7 copy-start.2
  3.8 1.2 %copy-start.1 = (bf16[512,4,256]{2,1,0:T(4,128)(2,1)S(1)}, bf16[512,4,256]{2,1,0:T(4,128)(2,1)}, u32[]{:S(2)}) copy-start(bf16[512,4,256]{2,1,0:T(4,128)(2,1)} %param.3) | copy-start | bytes 3145732
  5.6 1.1 %copy-start = (bf16[512,1024]{1,0:T(8,128)(2,1)}, bf16[512,1024]{1,0:T(8,128)(2,1)S(1)}, u32[]{:S(2)}) copy-start(bf16[512,1024]{1,0:T(8,128)(2,1)S(1)} %mul.16.kept) | copy-start | bytes 3145732

commit v2 on v1

v2 whole, which is shorter than its diff:
```python
import functools

import jax
import jax.numpy as jnp
from jax import lax
from jax.experimental import pallas as pl
from jax.experimental.pallas import tpu as pltpu
from jax.sharding import PartitionSpec as P

MESH = pl.DeviceIdType.MESH
NZH, NX, NCORE, NZL, NY = 4, 4, 2, 2, 8
NPB = 16
BLK = 128
K8 = 8
CHUNKS = 8
LANES = 4
TOP = 32767.0
LEVELS = 64.0
LN2 = 0.6931471805599453
AHEAD = {"across": 0, "relay": 4.5, "compact": 8, "share": 11.5, "share2": 15, "multiply": 17}
AFTER = {"hop1": 20.5, "hop2": 24, "hop3": 27.5, "merge": 31, "finish": 34.5}
SPACING = 20.0 / CHUNKS
RELAY_Z = [True] * CHUNKS
RELAY_X = [True] * CHUNKS
STRAIGHT = [t >= CHUNKS - 2 for t in range(CHUNKS)]
HOPS = 4
FULL = sum(4 if straight else 6 for straight in STRAIGHT)
LAST_SLOT = [2 * CHUNKS + sum(5 if s else 1 for s in STRAIGHT[:t]) for t in range(CHUNKS)]
HALF = 2 * CHUNKS + sum(5 if s else 1 for s in STRAIGHT)


def rank(zh, x, c):
    return (zh * NX + x) * NCORE + c


def wait_bytes(view, sem):
    pltpu.make_async_copy(view, view, sem).wait()


def encode(values, rows, scales, message):
    count = len(values)
    for i, value in enumerate(values):
        scales[pl.ds(i, 1), :] = jnp.max(jnp.abs(value), axis=0, keepdims=True)
    most = jnp.maximum(scales[...], 1e-33)
    level = jnp.floor(jnp.log(most) * (LEVELS / LN2)) + 2.0
    factor = jnp.exp(level * (-LN2 / LEVELS)) * TOP
    for i, value in enumerate(values):
        message[pl.ds(i * rows, rows), :] = jnp.round(value * factor[i : i + 1, :]).astype(jnp.int32).astype(jnp.int16)
    both = jnp.concatenate([level, jnp.zeros_like(level)], axis=0)
    message[pl.ds(count * rows, 16), :] = both.astype(jnp.int32).astype(jnp.int16)


def decode(message, rows, count):
    level = message[pl.ds(count * rows, 16), :].astype(jnp.int32).astype(jnp.float32)
    factor = jnp.exp(level * (LN2 / LEVELS)) * (1.0 / TOP)
    return [
        message[pl.ds(i * rows, rows), :].astype(jnp.int32).astype(jnp.float32) * factor[i : i + 1, :]
        for i in range(count)
    ]


def kernel(
    half, mask, blocks, mine_out, came_out, raw, land, kept, slot, panel, part,
    full_sent, full_got, half_sent, half_got, last_got, scales,
    s1s, s1r, s2s, s2n, s2f, s3s, s3n, s3f, s4s, s4r, full_s, half_s, rsr, fr, load, *stage,
):
    rows = BLK // CHUNKS
    b, a = lax.axis_index("basis"), lax.axis_index("aux")
    zh, x, c = b // (NX * NCORE), (b // NCORE) % NX, b % NCORE
    zl, y = a // NY, a % NY
    def at(zh_, x_, c_):
        return (rank(zh_, x_, c_), a)

    def up(y_, zl_=zl):
        return (b, zl_ * NY + y_)

    row_mates = [(dx, dc) for dx in (2, 1, 3, 0) for dc in range(NCORE) if dx or dc]
    barrier = pltpu.get_barrier_semaphore()
    mates = [at((zh + d) % NZH, x, c) for d in ((1, 3) if all(RELAY_Z) else (2, 1, 3))]
    mates += [up((y + d) % NY, 1 - zl) for d in ((1, NY - 1) if any(STRAIGHT) else ())]
    mates += [up((y + d) % NY) for d in (1, NY - 1)] + [up(y, 1 - zl)]
    mates += [at(zh, (x + dx) % NX, (c + dc) % NCORE) for dx, dc in row_mates]
    for mate in mates:
        pl.semaphore_signal(barrier, inc=1, device_id=mate, device_id_type=MESH)

    for w in range(4):
        pltpu.make_async_copy(half.at[pl.ds(w * BLK, BLK)], raw.at[w], load.at[w]).start()
    keeps = [[mask[0, o : o + 1, w : w + 1].astype(jnp.float32) for o in range(2)] for w in range(4)]
    within = jnp.int32(0)
    for j in range(NPB):
        within = within + jnp.where((blocks[j] >> 2) == b, blocks[j] & 3, 0)
    for w in range(4):
        wait_bytes(raw.at[w], load.at[w])

    def masked(block, keep):
        flat = block.reshape(BLK, 1024)
        both = jnp.concatenate([jnp.broadcast_to(k, (1, 128)) for k in keep] * 4, axis=1)
        return flat * both.astype(jnp.bfloat16)

    slot_keep = [sum(jnp.where(within == w, keeps[w][o], 0.0) for w in range(4)) for o in range(2)]
    slot[...] = masked(raw[within], slot_keep)
    pl.semaphore_wait(barrier, len(mates))

    def remote(src, dst, send, recv, mate):
        pltpu.make_async_remote_copy(
            src_ref=src, dst_ref=dst, send_sem=send, recv_sem=recv, device_id=mate, device_id_type=MESH
        ).start()

    eighth = 4 * c + x
    spans = [pl.ds(0, rows), pl.ds(rows, BLK - rows)]
    for i, span in enumerate(spans):
        for dx, dc in row_mates:
            x_, c_ = (x + dx) % NX, (c + dc) % NCORE
            lanes = pl.ds(pl.multiple_of((4 * c_ + x_) * 128, 128), 128)
            remote(slot.at[span, lanes], land.at[x * 2 + c, span], s1s.at[0], s1r.at[i], at(zh, x_, c_))
    land[x * 2 + c] = slot[:, pl.ds(pl.multiple_of(eighth * 128, 128), 128)]
    for w in range(4):
        kept[w] = masked(raw[w], keeps[w])

    def across(t):
        if t < 2:
            wait_bytes(land.at[pl.ds(0, 7), spans[t]], s1r.at[t])
        stage[t][pl.ds(zh * 8, 8)] = land[:, pl.ds(t * rows, rows)]
        mine = stage[t].at[pl.ds(zh * 8, 8)]
        remote(mine, mine, s2s.at[0], s2n.at[t], at((zh + 1) % NZH, x, c))
        remote(mine, mine, s2s.at[0], s2n.at[t], at((zh + 3) % NZH, x, c))
        if not RELAY_Z[t]:
            remote(mine, mine, s2s.at[0], s2f.at[t], at((zh + 2) % NZH, x, c))

    def relay(t):
        wait_bytes(stage[t].at[pl.ds(0, 16)], s2n.at[t])
        for i, d in enumerate((3, 1)):
            origin = ((zh + d) % NZH) * 8
            if RELAY_Z[t]:
                view = stage[t].at[pl.ds(origin + 4 * i, 4)]
                remote(view, view, s2s.at[0], s2f.at[t], at((zh + 4 - d) % NZH, x, c))

    def compact(t):
        wait_bytes(stage[t].at[pl.ds(((zh + 2) % NZH) * 8, 8)], s2f.at[t])
        for j in range(NPB):
            panel[t, eighth, pl.ds(j * rows, rows), :] = stage[t][blocks[j] >> 2]
        mine = panel.at[t, eighth]
        remote(mine, mine, s3s.at[0], s3n.at[t], at(zh, (x + 1) % NX, c))
        remote(mine, mine, s3s.at[0], s3n.at[t], at(zh, (x + 3) % NX, c))
        if not RELAY_X[t]:
            remote(mine, mine, s3s.at[0], s3f.at[t], at(zh, (x + 2) % NX, c))
        remote(mine, mine, s3s.at[0], s4r.at[t], at(zh, x, 1 - c))

    def share(t):
        wait_bytes(panel.at[t, pl.ds(0, 2)], s3n.at[t])
        for i, d in enumerate((3, 1)):
            origin = 4 * c + (x + d) % NX
            came = panel.at[t, origin]
            if RELAY_X[t]:
                view = panel.at[t, origin, pl.ds(8 * rows * i, 8 * rows)]
                remote(view, view, s3s.at[0], s3f.at[t], at(zh, (x + 4 - d) % NX, c))
            remote(came, came, s4s.at[0], s4r.at[t], at(zh, x, 1 - c))

    def share2(t):
        came = panel.at[t, 4 * c + (x + 2) % NX]
        wait_bytes(came, s3f.at[t])
        remote(came, came, s4s.at[0], s4r.at[t], at(zh, x, 1 - c))

    def multiply(t):
        wait_bytes(panel.at[t, pl.ds(0, 4)], s4r.at[t])
        lhs = jnp.concatenate([panel[t, k] for k in range(K8)], axis=1)
        value = lax.dot_general(
            lhs, kept[...].reshape(4 * BLK, 1024), (((1,), (1,)), ((), ())), preferred_element_type=jnp.float32
        )
        for g in range(LANES):
            part[t, g] = value[:, g * 128 : (g + 1) * 128].reshape(NPB, rows, 128)
        hop(t, 0)
        if STRAIGHT[t]:
            send_last(t, 2, 1 - zl, [part[t, g, y + NY * (1 - zl)] for g in range(LANES)])

    def slots(t, step):
        return 2 * t if step == 0 else 2 * (3 * t + step - 1)

    def gathered(t, step, way, halves):
        dest = (y + (HOPS - step) * (1 - 2 * way) + NY) % NY
        total = {(h, g): part[t, g, dest + NY * h] for h in halves for g in range(LANES)}
        if step == 0:
            return total
        for w in (0, 1) if step == HOPS else (way,):
            at_slot = slots(t, step - 1) + w
            message = half_got.at[at_slot] if step == 1 else full_got.at[at_slot]
            came_halves = [w] if step == 1 else [0, 1]
            came = decode(message, rows, LANES * len(came_halves))
            for i, h in enumerate(came_halves):
                for g in range(LANES):
                    total[h, g] = total[h, g] + came[i * LANES + g]
        return total

    def arrive(t, step):
        got = half_got if step == 0 else full_got
        wait_bytes(got.at[pl.ds(slots(t, step), 2)], rsr.at[t, step])

    def hop(t, step):
        if step:
            arrive(t, step - 1)
        for way in range(2):
            total = gathered(t, step, way, [way] if step == 0 else [0, 1])
            values = [v for _, v in sorted(total.items())]
            mate_y = (y + (1 if way == 0 else NY - 1)) % NY
            if step == HOPS - 1 and STRAIGHT[t]:
                for h in range(2):
                    send_last(t, way, h, values[LANES * h : LANES * h + LANES], mate_y)
                continue
            sent, got, sem = (half_sent, half_got, half_s) if step == 0 else (full_sent, full_got, full_s)
            at_slot = slots(t, step) + way
            encode(values, rows, scales, sent.at[at_slot])
            remote(sent.at[at_slot], got.at[at_slot], sem.at[0], rsr.at[t, step], up(mate_y))

    def send_last(t, way, h, values, mate_y=None):
        to = y if mate_y is None else mate_y
        at_slot = 4 if way == 2 else way + 2 * ((h + zl) % 2)
        number = LAST_SLOT[t] + (4 if way == 2 else way + 2 * h)
        message = half_sent.at[number]
        encode(values, rows, scales, message)
        remote(message, last_got.at[t, at_slot], half_s.at[0], fr.at[t], up(to, h))

    def merge(t):
        if STRAIGHT[t]:
            wait_bytes(last_got.at[t], fr.at[t])
            for g in range(LANES):
                mine_out[pl.ds(t * rows, rows), pl.ds(g * 128, 128)] = part[t, g, y + NY * zl]
            came = [decode(last_got.at[t, i], rows, LANES) for i in range(5)]
            for g in range(LANES):
                came_out[pl.ds(t * rows, rows), pl.ds(g * 128, 128)] = sum(part_[g] for part_ in came)
            return
        arrive(t, HOPS - 1)
        total = gathered(t, HOPS, 0, [0, 1])
        away = [jnp.where(zl == 0, total[1, g], total[0, g]) for g in range(LANES)]
        for g in range(LANES):
            lanes = pl.ds(g * 128, 128)
            mine_out[pl.ds(t * rows, rows), lanes] = jnp.where(zl == 0, total[0, g], total[1, g])
        message = half_sent.at[LAST_SLOT[t]]
        encode(away, rows, scales, message)
        remote(message, last_got.at[t, 4], half_s.at[0], fr.at[t], up(y, 1 - zl))

    def finish(t):
        if STRAIGHT[t]:
            return
        wait_bytes(last_got.at[t, 4], fr.at[t])
        for g, value in enumerate(decode(last_got.at[t, 4], rows, LANES)):
            came_out[pl.ds(t * rows, rows), pl.ds(g * 128, 128)] = value

    work = {
        "across": across, "relay": relay, "compact": compact, "share": share, "share2": share2, "multiply": multiply,
        "hop1": lambda t: hop(t, 1), "hop2": lambda t: hop(t, 2), "hop3": lambda t: hop(t, 3),
        "merge": merge, "finish": finish,
    }
    when = []
    for t in range(CHUNKS):
        plan = AHEAD | AFTER
        when += [(plan[name] + SPACING * t, i, t, name) for i, name in enumerate(work)]
    for _, _, t, name in sorted(when):
        work[name](t)

    wait_bytes(land.at[pl.ds(0, 7)], s1s.at[0])
    wait_bytes(panel.at[pl.ds(0, CHUNKS // 2), pl.ds(0, 3)], s2s.at[0])
    wait_bytes(panel.at[:, pl.ds(0, 4)], s3s.at[0])
    wait_bytes(panel.at[:, pl.ds(0, 3)], s4s.at[0])
    wait_bytes(full_sent.at[pl.ds(0, FULL)], full_s.at[0])
    wait_bytes(half_sent, half_s.at[0])


def body(half_three, block_mask, panel_blocks):
    cols, auxw, occ = half_three.shape
    width = auxw * occ
    rows = BLK // CHUNKS
    dma = pltpu.SemaphoreType.DMA
    vmem = pltpu.VMEM
    mine, came = pl.pallas_call(
        kernel,
        out_shape=[jax.ShapeDtypeStruct((BLK, cols), jnp.float32)] * 2,
        in_specs=[
            pl.BlockSpec(memory_space=pltpu.HBM),
            pl.BlockSpec(memory_space=pltpu.VMEM),
            pl.BlockSpec(memory_space=pltpu.SMEM),
        ],
        out_specs=[pl.BlockSpec(memory_space=pltpu.VMEM)] * 2,
        scratch_shapes=[
            vmem((4, BLK, auxw, occ), jnp.bfloat16),
            vmem((8, BLK, 128), jnp.bfloat16),
            vmem((4, BLK, width), jnp.bfloat16),
            vmem((BLK, width), jnp.bfloat16),
            vmem((CHUNKS, K8, NPB * rows, 128), jnp.bfloat16),
            vmem((CHUNKS, LANES, NPB, rows, 128), jnp.float32),
            vmem((6 * CHUNKS, 8 * rows + 16, 128), jnp.int16),
            vmem((6 * CHUNKS, 8 * rows + 16, 128), jnp.int16),
            vmem((HALF, 4 * rows + 16, 128), jnp.int16),
            vmem((2 * CHUNKS, 4 * rows + 16, 128), jnp.int16),
            vmem((CHUNKS, 5, 4 * rows + 16, 128), jnp.int16),
            vmem((8, 128), jnp.float32),
            dma((1,)), dma((2,)), dma((1,)), dma((CHUNKS,)), dma((CHUNKS,)),
            dma((1,)), dma((CHUNKS,)), dma((CHUNKS,)), dma((1,)), dma((CHUNKS,)),
            dma((1,)), dma((1,)), dma((CHUNKS, HOPS)), dma((CHUNKS,)), dma((4,)),
            *[vmem((32, rows, 128), jnp.bfloat16) for _ in range(CHUNKS)],
        ],
        compiler_params=pltpu.CompilerParams(
            collective_id=0, has_side_effects=True, vmem_limit_bytes=24 << 20
        ),
        cost_estimate=pl.CostEstimate(flops=2 * 2048 * cols * width, bytes_accessed=2 << 20, transcendentals=0),
    )(half_three, block_mask.transpose(1, 2, 0), panel_blocks)
    return mine + came


def solution(mesh):
    placed = (P("basis", "aux", None), P("basis", "aux", None), P())
    return jax.shard_map(
        body, mesh=mesh, in_specs=placed, out_specs=P("aux", "basis"), check_vma=False
    )
```

time: 93.7 us -> 75 us (0.80)
  Pallas kernels: 85.1 us -> 72.2 us
  local copies, waits for them, and re-layouts: 6.12 us -> 1.92 us
    pallas_call x1, Pallas kernels: 85.1 us -> 72.2 us  [body(): pl.pallas_call(kernel, out_shape=[jax.ShapeDtypeStruct((BLK, cols), jnp.f...]
    unnamed x10 -> x6, local copies, waits for them, and re-layouts: 3.85 us -> 1.92 us
    mul x2 -> x0, local copies, waits for them, and re-layouts: 1.37 us -> none  [body(): kept = (shaped * keep).reshape(cols, width)]
    reduce_sum x1 -> x0, other arithmetic: 1.15 us -> none  [body(): within = jnp.sum(jnp.where(mine, panel_blocks % nbb, 0))]
where the time goes in v2:
time: 75 us; the launch traced here: 74.8 us
  Pallas kernels  72.2 us (96%)
  local copies, waits for them, and re-layouts  1.92 us (3%)
    pallas_call x1, Pallas kernels, body(): pl.pallas_call(kernel, out_shape=[jax.ShapeDtypeStruct((BLK, cols), jnp.f...  72.2 us
    unnamed x6, local copies, waits for them, and re-layouts  1.92 us

profile of v2, /device:TPU:16, one launch (start us, length us, event | category | flops | bytes accessed | tf_op | source)
XLA Modules:
  0.0 74.8 jit_solution(15063035029785491720)
XLA Ops:
  0.0 0.0 copy-start.2
  0.0 0.0 copy-start.1
  0.0 0.7 copy-done.2
  0.7 0.0 copy-done.1
  0.7 0.0 copy-start
  0.7 1.2 %copy-done = bf16[512,4,256]{2,1,0:T(4,128)(2,1)S(1)} copy-done((bf16[512,4,256]{2,1,0:T(4,128)(2,1)S(1)}, bf16[512,4,256]{2,1,0:T(4,128)(2,1)}, u32[]{:S(2)}) %copy-start) | copy-done | bytes 1048600
  1.9 72.2 %shard_map.37 = (f32[128,512]{1,0:T(8,128)S(1)}, f32[128,512]{1,0:T(8,128)S(1)}) custom-call(bf16[512,4,256]{2,1,0:T(4,128)(2,1)S(1)} %copy-done, s32[1,2,4]{2,1,0:T(2,128)S(1)} %bitcast.1, s32[16]{0:T(128)S(1)} %copy-done.2), custom_call_target="tpu_custom_call" | custom-call | flops 2147483648 | bytes 2097152 | tf_op jit(solution)/shard_map/pallas_call | solution.py:274
  74.1 0.7 add.3
Async XLA Ops:
  0.0 0.7 copy-start.2
  0.0 0.7 copy-start.1
  0.7 1.2 %copy-start = (bf16[512,4,256]{2,1,0:T(4,128)(2,1)S(1)}, bf16[512,4,256]{2,1,0:T(4,128)(2,1)}, u32[]{:S(2)}) copy-start(bf16[512,4,256]{2,1,0:T(4,128)(2,1)} %half.1) | copy-start | bytes 3145732

commit v3 on v2

--- a/solution.py
+++ b/solution.py
@@ -15,16 +15,15 @@
 CHUNKS = 8
 LANES = 4
 TOP = 32767.0
-LEVELS = 64.0
-LN2 = 0.6931471805599453
 AHEAD = {"across": 0, "relay": 4.5, "compact": 8, "share": 11.5, "share2": 15, "multiply": 17}
 AFTER = {"hop1": 20.5, "hop2": 24, "hop3": 27.5, "merge": 31, "finish": 34.5}
-SPACING = 20.0 / CHUNKS
+SPACING = 14.0 / CHUNKS
 RELAY_Z = [True] * CHUNKS
-RELAY_X = [True] * CHUNKS
+RELAY_X = [t > 0 for t in range(CHUNKS)]
 STRAIGHT = [t >= CHUNKS - 2 for t in range(CHUNKS)]
 HOPS = 4
 FULL = sum(4 if straight else 6 for straight in STRAIGHT)
+FULL_SLOT = [sum(4 if s else 6 for s in STRAIGHT[:t]) for t in range(CHUNKS)]
 LAST_SLOT = [2 * CHUNKS + sum(5 if s else 1 for s in STRAIGHT[:t]) for t in range(CHUNKS)]
 HALF = 2 * CHUNKS + sum(5 if s else 1 for s in STRAIGHT)
 
@@ -37,32 +36,31 @@
     pltpu.make_async_copy(view, view, sem).wait()
 
 
-def encode(values, rows, scales, message):
-    count = len(values)
-    for i, value in enumerate(values):
-        scales[pl.ds(i, 1), :] = jnp.max(jnp.abs(value), axis=0, keepdims=True)
-    most = jnp.maximum(scales[...], 1e-33)
-    level = jnp.floor(jnp.log(most) * (LEVELS / LN2)) + 2.0
-    factor = jnp.exp(level * (-LN2 / LEVELS)) * TOP
-    for i, value in enumerate(values):
-        message[pl.ds(i * rows, rows), :] = jnp.round(value * factor[i : i + 1, :]).astype(jnp.int32).astype(jnp.int16)
-    both = jnp.concatenate([level, jnp.zeros_like(level)], axis=0)
-    message[pl.ds(count * rows, 16), :] = both.astype(jnp.int32).astype(jnp.int16)
-
-
-def decode(message, rows, count):
-    level = message[pl.ds(count * rows, 16), :].astype(jnp.int32).astype(jnp.float32)
-    factor = jnp.exp(level * (LN2 / LEVELS)) * (1.0 / TOP)
+def encode(values, rows, message, scale):
+    for n in range(0, len(values), LANES):
+        block = values[n : n + LANES]
+        most = functools.reduce(jnp.maximum, [jnp.abs(value) for value in block])
+        most = jnp.maximum(jnp.max(most, axis=0, keepdims=True), 1e-33)
+        scale[n // LANES] = most
+        factor = TOP / most
+        for i, value in enumerate(block):
+            coded = jnp.round(value * factor).astype(jnp.int32).astype(jnp.int16)
+            message[pl.ds((n + i) * rows, rows), :] = coded
+
+
+def decode(message, scale, rows, count):
+    factors = [scale[n] * (1.0 / TOP) for n in range(count // LANES)]
     return [
-        message[pl.ds(i * rows, rows), :].astype(jnp.int32).astype(jnp.float32) * factor[i : i + 1, :]
+        message[pl.ds(i * rows, rows), :].astype(jnp.int32).astype(jnp.float32) * factors[i // LANES]
         for i in range(count)
     ]
 
 
 def kernel(
     half, mask, blocks, mine_out, came_out, raw, land, kept, slot, panel, part,
-    full_sent, full_got, half_sent, half_got, last_got, scales,
-    s1s, s1r, s2s, s2n, s2f, s3s, s3n, s3f, s4s, s4r, full_s, half_s, rsr, fr, load, *stage,
+    full_sent, full_got, half_sent, half_got, last_got,
+    scale_sent, full_scale, half_scale, last_scale, tally,
+    s1s, s1r, s2s, s2n, s2f, s3s, s3n, s3f, s4s, s4r, full_s, half_s, scale_s, rsr, fr, load, *stage,
 ):
     rows = BLK // CHUNKS
     b, a = lax.axis_index("basis"), lax.axis_index("aux")
@@ -173,8 +171,10 @@
         if STRAIGHT[t]:
             send_last(t, 2, 1 - zl, [part[t, g, y + NY * (1 - zl)] for g in range(LANES)])
 
+    full_rows, half_rows = 4 * rows + 2, 2 * rows + 1
+
     def slots(t, step):
-        return 2 * t if step == 0 else 2 * (3 * t + step - 1)
+        return 2 * t if step == 0 else FULL_SLOT[t] + 2 * (step - 1)
 
     def gathered(t, step, way, halves):
         dest = (y + (HOPS - step) * (1 - 2 * way) + NY) % NY
@@ -183,17 +183,16 @@
             return total
         for w in (0, 1) if step == HOPS else (way,):
             at_slot = slots(t, step - 1) + w
-            message = half_got.at[at_slot] if step == 1 else full_got.at[at_slot]
+            got, scale = (half_got, half_scale) if step == 1 else (full_got, full_scale)
             came_halves = [w] if step == 1 else [0, 1]
-            came = decode(message, rows, LANES * len(came_halves))
+            came = decode(got.at[at_slot], scale.at[at_slot], rows, LANES * len(came_halves))
             for i, h in enumerate(came_halves):
                 for g in range(LANES):
                     total[h, g] = total[h, g] + came[i * LANES + g]
         return total
 
     def arrive(t, step):
-        got = half_got if step == 0 else full_got
-        wait_bytes(got.at[pl.ds(slots(t, step), 2)], rsr.at[t, step])
+        wait_bytes(tally.at[pl.ds(0, 2 * (half_rows if step == 0 else full_rows))], rsr.at[t, step])
 
     def hop(t, step):
         if step:
@@ -206,25 +205,29 @@
                 for h in range(2):
                     send_last(t, way, h, values[LANES * h : LANES * h + LANES], mate_y)
                 continue
-            sent, got, sem = (half_sent, half_got, half_s) if step == 0 else (full_sent, full_got, full_s)
             at_slot = slots(t, step) + way
-            encode(values, rows, scales, sent.at[at_slot])
-            remote(sent.at[at_slot], got.at[at_slot], sem.at[0], rsr.at[t, step], up(mate_y))
+            if step == 0:
+                send(values, half_sent.at[at_slot], pl.ds(2 * FULL + at_slot, 1), half_got, half_scale, at_slot, half_s, rsr.at[t, step], up(mate_y))
+            else:
+                send(values, full_sent.at[at_slot], pl.ds(2 * at_slot, 2), full_got, full_scale, at_slot, full_s, rsr.at[t, step], up(mate_y))
+
+    def send(values, message, number, got, got_scale, where, sem, recv, mate):
+        encode(values, rows, message, scale_sent.at[number])
+        remote(message, got.at[where], sem.at[0], recv, mate)
+        remote(scale_sent.at[number], got_scale.at[where], scale_s.at[0], recv, mate)
 
     def send_last(t, way, h, values, mate_y=None):
         to = y if mate_y is None else mate_y
         at_slot = 4 if way == 2 else way + 2 * ((h + zl) % 2)
         number = LAST_SLOT[t] + (4 if way == 2 else way + 2 * h)
-        message = half_sent.at[number]
-        encode(values, rows, scales, message)
-        remote(message, last_got.at[t, at_slot], half_s.at[0], fr.at[t], up(to, h))
+        send(values, half_sent.at[number], pl.ds(2 * FULL + number, 1), last_got.at[t], last_scale.at[t], at_slot, half_s, fr.at[t], up(to, h))
 
     def merge(t):
         if STRAIGHT[t]:
-            wait_bytes(last_got.at[t], fr.at[t])
+            wait_bytes(tally.at[pl.ds(0, 5 * half_rows)], fr.at[t])
             for g in range(LANES):
                 mine_out[pl.ds(t * rows, rows), pl.ds(g * 128, 128)] = part[t, g, y + NY * zl]
-            came = [decode(last_got.at[t, i], rows, LANES) for i in range(5)]
+            came = [decode(last_got.at[t, i], last_scale.at[t, i], rows, LANES) for i in range(5)]
             for g in range(LANES):
                 came_out[pl.ds(t * rows, rows), pl.ds(g * 128, 128)] = sum(part_[g] for part_ in came)
             return
@@ -234,15 +237,14 @@
         for g in range(LANES):
             lanes = pl.ds(g * 128, 128)
             mine_out[pl.ds(t * rows, rows), lanes] = jnp.where(zl == 0, total[0, g], total[1, g])
-        message = half_sent.at[LAST_SLOT[t]]
-        encode(away, rows, scales, message)
-        remote(message, last_got.at[t, 4], half_s.at[0], fr.at[t], up(y, 1 - zl))
+        number = LAST_SLOT[t]
+        send(away, half_sent.at[number], pl.ds(2 * FULL + number, 1), last_got.at[t], last_scale.at[t], 4, half_s, fr.at[t], up(y, 1 - zl))
 
     def finish(t):
         if STRAIGHT[t]:
             return
-        wait_bytes(last_got.at[t, 4], fr.at[t])
-        for g, value in enumerate(decode(last_got.at[t, 4], rows, LANES)):
+        wait_bytes(tally.at[pl.ds(0, half_rows)], fr.at[t])
+        for g, value in enumerate(decode(last_got.at[t, 4], last_scale.at[t, 4], rows, LANES)):
             came_out[pl.ds(t * rows, rows), pl.ds(g * 128, 128)] = value
 
     work = {
@@ -261,8 +263,9 @@
     wait_bytes(panel.at[pl.ds(0, CHUNKS // 2), pl.ds(0, 3)], s2s.at[0])
     wait_bytes(panel.at[:, pl.ds(0, 4)], s3s.at[0])
     wait_bytes(panel.at[:, pl.ds(0, 3)], s4s.at[0])
-    wait_bytes(full_sent.at[pl.ds(0, FULL)], full_s.at[0])
+    wait_bytes(full_sent, full_s.at[0])
     wait_bytes(half_sent, half_s.at[0])
+    wait_bytes(scale_sent, scale_s.at[0])
 
 
 def body(half_three, block_mask, panel_blocks):
@@ -287,15 +290,19 @@
             vmem((BLK, width), jnp.bfloat16),
             vmem((CHUNKS, K8, NPB * rows, 128), jnp.bfloat16),
             vmem((CHUNKS, LANES, NPB, rows, 128), jnp.float32),
-            vmem((6 * CHUNKS, 8 * rows + 16, 128), jnp.int16),
-            vmem((6 * CHUNKS, 8 * rows + 16, 128), jnp.int16),
-            vmem((HALF, 4 * rows + 16, 128), jnp.int16),
-            vmem((2 * CHUNKS, 4 * rows + 16, 128), jnp.int16),
-            vmem((CHUNKS, 5, 4 * rows + 16, 128), jnp.int16),
-            vmem((8, 128), jnp.float32),
+            vmem((FULL, 8 * rows, 128), jnp.int16),
+            vmem((FULL, 8 * rows, 128), jnp.int16),
+            vmem((HALF, 4 * rows, 128), jnp.int16),
+            vmem((2 * CHUNKS, 4 * rows, 128), jnp.int16),
+            vmem((CHUNKS, 5, 4 * rows, 128), jnp.int16),
+            vmem((2 * FULL + HALF, 1, 128), jnp.float32),
+            vmem((FULL, 2, 1, 128), jnp.float32),
+            vmem((2 * CHUNKS, 1, 1, 128), jnp.float32),
+            vmem((CHUNKS, 5, 1, 1, 128), jnp.float32),
+            vmem((5 * (2 * rows + 1), 1, 128), jnp.float32),
             dma((1,)), dma((2,)), dma((1,)), dma((CHUNKS,)), dma((CHUNKS,)),
             dma((1,)), dma((CHUNKS,)), dma((CHUNKS,)), dma((1,)), dma((CHUNKS,)),
-            dma((1,)), dma((1,)), dma((CHUNKS, HOPS)), dma((CHUNKS,)), dma((4,)),
+            dma((1,)), dma((1,)), dma((1,)), dma((CHUNKS, HOPS)), dma((CHUNKS,)), dma((4,)),
             *[vmem((32, rows, 128), jnp.bfloat16) for _ in range(CHUNKS)],
         ],
         compiler_params=pltpu.CompilerParams(

time: 75 us -> 71.5 us (0.953)
  Pallas kernels: 72.2 us -> 68.7 us
    pallas_call x1, Pallas kernels: 72.2 us -> 68.7 us  [body(): pl.pallas_call(kernel, out_shape=[jax.ShapeDtypeStruct((BLK, cols), jnp.f...]
where the time goes in v3:
time: 71.5 us; the launch traced here: 71.4 us
  Pallas kernels  68.7 us (96%)
  local copies, waits for them, and re-layouts  1.92 us (3%)
  other arithmetic  0.74 us (1%)
    pallas_call x1, Pallas kernels, body(): pl.pallas_call(kernel, out_shape=[jax.ShapeDtypeStruct((BLK, cols), jnp.f...  68.7 us
    unnamed x6, local copies, waits for them, and re-layouts  1.92 us

profile of v3, /device:TPU:16, one launch (start us, length us, event | category | flops | bytes accessed | tf_op | source)
XLA Modules:
  0.0 71.4 jit_solution(884586841931031977)
XLA Ops:
  0.0 0.0 copy-start.2
  0.0 0.0 copy-start.1
  0.0 0.7 copy-done.2
  0.7 0.0 copy-done.1
  0.7 0.0 copy-start
  0.7 1.2 %copy-done = bf16[512,4,256]{2,1,0:T(4,128)(2,1)S(1)} copy-done((bf16[512,4,256]{2,1,0:T(4,128)(2,1)S(1)}, bf16[512,4,256]{2,1,0:T(4,128)(2,1)}, u32[]{:S(2)}) %copy-start) | copy-done | bytes 1048600
  1.9 68.7 %shard_map.37 = (f32[128,512]{1,0:T(8,128)S(1)}, f32[128,512]{1,0:T(8,128)S(1)}) custom-call(bf16[512,4,256]{2,1,0:T(4,128)(2,1)S(1)} %copy-done, s32[1,2,4]{2,1,0:T(2,128)S(1)} %bitcast.1, s32[16]{0:T(128)S(1)} %copy-done.2), custom_call_target="tpu_custom_call" | custom-call | flops 2147483648 | bytes 2097152 | tf_op jit(solution)/shard_map/pallas_call | solution.py:277
  70.6 0.7 %add.3 = f32[128,512]{1,0:T(8,128)} add(f32[128,512]{1,0:T(8,128)S(1)} %get-tuple-element.7, f32[128,512]{1,0:T(8,128)S(1)} %get-tuple-element.8) | non-fusion elementwise | flops 65536 | bytes 786432 | tf_op jit(solution)/shard_map/add | solution.py:313
Async XLA Ops:
  0.0 0.7 copy-start.2
  0.0 0.7 copy-start.1
  0.7 1.2 %copy-start = (bf16[512,4,256]{2,1,0:T(4,128)(2,1)S(1)}, bf16[512,4,256]{2,1,0:T(4,128)(2,1)}, u32[]{:S(2)}) copy-start(bf16[512,4,256]{2,1,0:T(4,128)(2,1)} %half.1) | copy-start | bytes 3145732

commit v4 on v3

--- a/solution.py
+++ b/solution.py
@@ -57,10 +57,10 @@
 
 
 def kernel(
-    half, mask, blocks, mine_out, came_out, raw, land, kept, slot, panel, part,
+    half, mask_in, blocks_in, mine_out, came_out, raw, land, kept, slot, panel, part,
     full_sent, full_got, half_sent, half_got, last_got,
     scale_sent, full_scale, half_scale, last_scale, tally,
-    s1s, s1r, s2s, s2n, s2f, s3s, s3n, s3f, s4s, s4r, full_s, half_s, scale_s, rsr, fr, load, *stage,
+    s1s, s1r, s2s, s2n, s2f, s3s, s3n, s3f, s4s, s4r, full_s, half_s, scale_s, rsr, fr, load, mask, blocks, *stage,
 ):
     rows = BLK // CHUNKS
     b, a = lax.axis_index("basis"), lax.axis_index("aux")
@@ -81,8 +81,13 @@
     for mate in mates:
         pl.semaphore_signal(barrier, inc=1, device_id=mate, device_id_type=MESH)
 
+    small = [pltpu.make_async_copy(mask_in, mask, load.at[4]), pltpu.make_async_copy(blocks_in, blocks, load.at[5])]
+    for copy in small:
+        copy.start()
     for w in range(4):
         pltpu.make_async_copy(half.at[pl.ds(w * BLK, BLK)], raw.at[w], load.at[w]).start()
+    for copy in small:
+        copy.wait()
     keeps = [[mask[0, o : o + 1, w : w + 1].astype(jnp.float32) for o in range(2)] for w in range(4)]
     within = jnp.int32(0)
     for j in range(NPB):
@@ -279,8 +284,8 @@
         out_shape=[jax.ShapeDtypeStruct((BLK, cols), jnp.float32)] * 2,
         in_specs=[
             pl.BlockSpec(memory_space=pltpu.HBM),
-            pl.BlockSpec(memory_space=pltpu.VMEM),
-            pl.BlockSpec(memory_space=pltpu.SMEM),
+            pl.BlockSpec(memory_space=pltpu.HBM),
+            pl.BlockSpec(memory_space=pltpu.HBM),
         ],
         out_specs=[pl.BlockSpec(memory_space=pltpu.VMEM)] * 2,
         scratch_shapes=[
@@ -302,14 +307,15 @@
             vmem((5 * (2 * rows + 1), 1, 128), jnp.float32),
             dma((1,)), dma((2,)), dma((1,)), dma((CHUNKS,)), dma((CHUNKS,)),
             dma((1,)), dma((CHUNKS,)), dma((CHUNKS,)), dma((1,)), dma((CHUNKS,)),
-            dma((1,)), dma((1,)), dma((1,)), dma((CHUNKS, HOPS)), dma((CHUNKS,)), dma((4,)),
+            dma((1,)), dma((1,)), dma((1,)), dma((CHUNKS, HOPS)), dma((CHUNKS,)), dma((6,)),
+            vmem((1, 2, 4), jnp.int32), pltpu.SMEM((NPB,), jnp.int32),
             *[vmem((32, rows, 128), jnp.bfloat16) for _ in range(CHUNKS)],
         ],
         compiler_params=pltpu.CompilerParams(
             collective_id=0, has_side_effects=True, vmem_limit_bytes=24 << 20
         ),
         cost_estimate=pl.CostEstimate(flops=2 * 2048 * cols * width, bytes_accessed=2 << 20, transcendentals=0),
-    )(half_three, block_mask.transpose(1, 2, 0), panel_blocks)
+    )(pltpu.with_memory_space_constraint(half_three, pltpu.HBM), pltpu.with_memory_space_constraint(block_mask.transpose(1, 2, 0), pltpu.HBM), pltpu.with_memory_space_constraint(panel_blocks, pltpu.HBM))
     return mine + came
 
 

time: 71.5 us -> 69.2 us (0.968)
  the two profiles are of different devices: /device:TPU:16 before, /device:TPU:24 now
where the time goes in v4:
time: 69.2 us; the launch traced here: 69.1 us
  Pallas kernels  68.4 us (99%)
  other arithmetic  0.74 us (1%)
    pallas_call x1, Pallas kernels, body(): pl.pallas_call(kernel, out_shape=[jax.ShapeDtypeStruct((BLK, cols), jnp.f...  68.4 us

profile of v4, /device:TPU:24, one launch (start us, length us, event | category | flops | bytes accessed | tf_op | source)
XLA Modules:
  0.0 69.1 jit_solution(7369826118281337298)
XLA Ops:
  0.0 68.4 %shard_map.37 = (f32[128,512]{1,0:T(8,128)S(1)}, f32[128,512]{1,0:T(8,128)S(1)}) custom-call(bf16[512,4,256]{2,1,0:T(4,128)(2,1)} %half.1, s32[1,2,4]{2,1,0:T(2,128)} %bitcast.1, s32[16]{0:T(128)} %blocks_in.1), custom_call_target="tpu_custom_call" | custom-call | flops 2147483648 | bytes 2097152 | tf_op jit(solution)/shard_map/pallas_call | solution.py:282
  68.4 0.7 %add.3 = f32[128,512]{1,0:T(8,128)} add(f32[128,512]{1,0:T(8,128)S(1)} %get-tuple-element.7, f32[128,512]{1,0:T(8,128)S(1)} %get-tuple-element.8) | non-fusion elementwise | flops 65536 | bytes 786432 | tf_op jit(solution)/shard_map/add | solution.py:319

commit v5 on v4

--- a/solution.py
+++ b/solution.py
@@ -15,11 +15,18 @@
 CHUNKS = 8
 LANES = 4
 TOP = 32767.0
-AHEAD = {"across": 0, "relay": 4.5, "compact": 8, "share": 11.5, "share2": 15, "multiply": 17}
-AFTER = {"hop1": 20.5, "hop2": 24, "hop3": 27.5, "merge": 31, "finish": 34.5}
-SPACING = 14.0 / CHUNKS
+ORDER = [
+    (0, 0), (0, 1), (0, 4), (1, 0), (0, 2), (1, 1), (1, 4), (0, 5), (2, 0), (1, 2), (0, 3),
+    (2, 1), (0, 7), (2, 4), (3, 0), (1, 5), (2, 2), (0, 6), (1, 3), (3, 1), (3, 4), (2, 5),
+    (1, 7), (4, 0), (1, 6), (3, 2), (5, 0), (4, 1), (2, 3), (4, 4), (5, 1), (3, 5), (2, 7),
+    (5, 4), (6, 0), (4, 2), (2, 6), (5, 2), (6, 1), (3, 3), (4, 5), (6, 4), (7, 0), (3, 7),
+    (5, 5), (3, 6), (6, 2), (4, 3), (7, 1), (7, 4), (5, 3), (4, 7), (6, 5), (4, 6), (8, 0),
+    (5, 7), (5, 6), (8, 1), (6, 3), (7, 5), (6, 7), (6, 6), (7, 2), (9, 1), (7, 3), (8, 5),
+    (7, 7), (7, 6), (8, 4), (10, 1), (8, 2), (8, 3), (9, 0), (9, 5), (8, 7), (8, 6), (9, 4),
+    (9, 2), (9, 3), (9, 7), (10, 7), (10, 4), (9, 6), (10, 0), (10, 2), (10, 5), (10, 3), (10, 6),
+]
 RELAY_Z = [True] * CHUNKS
-RELAY_X = [t > 0 for t in range(CHUNKS)]
+RELAY_X = [True] * CHUNKS
 STRAIGHT = [t >= CHUNKS - 2 for t in range(CHUNKS)]
 HOPS = 4
 FULL = sum(4 if straight else 6 for straight in STRAIGHT)
@@ -257,12 +264,9 @@
         "hop1": lambda t: hop(t, 1), "hop2": lambda t: hop(t, 2), "hop3": lambda t: hop(t, 3),
         "merge": merge, "finish": finish,
     }
-    when = []
-    for t in range(CHUNKS):
-        plan = AHEAD | AFTER
-        when += [(plan[name] + SPACING * t, i, t, name) for i, name in enumerate(work)]
-    for _, _, t, name in sorted(when):
-        work[name](t)
+    names = list(work)
+    for stage_number, t in ORDER:
+        work[names[stage_number]](t)
 
     wait_bytes(land.at[pl.ds(0, 7)], s1s.at[0])
     wait_bytes(panel.at[pl.ds(0, CHUNKS // 2), pl.ds(0, 3)], s2s.at[0])

time: 69.2 us -> 67.4 us (0.974)
  the two profiles are of different devices: /device:TPU:24 before, /device:TPU:16 now
where the time goes in v5:
time: 67.4 us; the launch traced here: 67.3 us
  Pallas kernels  66.5 us (99%)
  other arithmetic  0.74 us (1%)
    pallas_call x1, Pallas kernels, body(): pl.pallas_call(kernel, out_shape=[jax.ShapeDtypeStruct((BLK, cols), jnp.f...  66.5 us

profile of v5, /device:TPU:16, one launch (start us, length us, event | category | flops | bytes accessed | tf_op | source)
XLA Modules:
  0.0 67.3 jit_solution(1333895100368582154)
XLA Ops:
  0.0 66.5 %shard_map.37 = (f32[128,512]{1,0:T(8,128)S(1)}, f32[128,512]{1,0:T(8,128)S(1)}) custom-call(bf16[512,4,256]{2,1,0:T(4,128)(2,1)} %half.1, s32[1,2,4]{2,1,0:T(2,128)} %bitcast.1, s32[16]{0:T(128)} %blocks_in.1), custom_call_target="tpu_custom_call" | custom-call | flops 2147483648 | bytes 2097152 | tf_op jit(solution)/shard_map/pallas_call | solution.py:286
  66.5 0.7 %add.3 = f32[128,512]{1,0:T(8,128)} add(f32[128,512]{1,0:T(8,128)S(1)} %get-tuple-element.7, f32[128,512]{1,0:T(8,128)S(1)} %get-tuple-element.8) | non-fusion elementwise | flops 65536 | bytes 786432 | tf_op jit(solution)/shard_map/add | solution.py:323

commit v6 on v5

--- a/solution.py
+++ b/solution.py
@@ -64,7 +64,7 @@
 
 
 def kernel(
-    half, mask_in, blocks_in, mine_out, came_out, raw, land, kept, slot, panel, part,
+    half, mask_in, blocks_in, out, raw, land, kept, slot, panel, part,
     full_sent, full_got, half_sent, half_got, last_got,
     scale_sent, full_scale, half_scale, last_scale, tally,
     s1s, s1r, s2s, s2n, s2f, s3s, s3n, s3f, s4s, s4r, full_s, half_s, scale_s, rsr, fr, load, mask, blocks, *stage,
@@ -237,18 +237,16 @@
     def merge(t):
         if STRAIGHT[t]:
             wait_bytes(tally.at[pl.ds(0, 5 * half_rows)], fr.at[t])
-            for g in range(LANES):
-                mine_out[pl.ds(t * rows, rows), pl.ds(g * 128, 128)] = part[t, g, y + NY * zl]
             came = [decode(last_got.at[t, i], last_scale.at[t, i], rows, LANES) for i in range(5)]
             for g in range(LANES):
-                came_out[pl.ds(t * rows, rows), pl.ds(g * 128, 128)] = sum(part_[g] for part_ in came)
+                out[pl.ds(t * rows, rows), pl.ds(g * 128, 128)] = part[t, g, y + NY * zl] + sum(part_[g] for part_ in came)
             return
         arrive(t, HOPS - 1)
         total = gathered(t, HOPS, 0, [0, 1])
         away = [jnp.where(zl == 0, total[1, g], total[0, g]) for g in range(LANES)]
         for g in range(LANES):
             lanes = pl.ds(g * 128, 128)
-            mine_out[pl.ds(t * rows, rows), lanes] = jnp.where(zl == 0, total[0, g], total[1, g])
+            out[pl.ds(t * rows, rows), lanes] = jnp.where(zl == 0, total[0, g], total[1, g])
         number = LAST_SLOT[t]
         send(away, half_sent.at[number], pl.ds(2 * FULL + number, 1), last_got.at[t], last_scale.at[t], 4, half_s, fr.at[t], up(y, 1 - zl))
 
@@ -257,7 +255,7 @@
             return
         wait_bytes(tally.at[pl.ds(0, half_rows)], fr.at[t])
         for g, value in enumerate(decode(last_got.at[t, 4], last_scale.at[t, 4], rows, LANES)):
-            came_out[pl.ds(t * rows, rows), pl.ds(g * 128, 128)] = value
+            out[pl.ds(t * rows, rows), pl.ds(g * 128, 128)] += value
 
     work = {
         "across": across, "relay": relay, "compact": compact, "share": share, "share2": share2, "multiply": multiply,
@@ -283,15 +281,15 @@
     rows = BLK // CHUNKS
     dma = pltpu.SemaphoreType.DMA
     vmem = pltpu.VMEM
-    mine, came = pl.pallas_call(
+    return pl.pallas_call(
         kernel,
-        out_shape=[jax.ShapeDtypeStruct((BLK, cols), jnp.float32)] * 2,
+        out_shape=jax.ShapeDtypeStruct((BLK, cols), jnp.float32),
         in_specs=[
             pl.BlockSpec(memory_space=pltpu.HBM),
             pl.BlockSpec(memory_space=pltpu.HBM),
             pl.BlockSpec(memory_space=pltpu.HBM),
         ],
-        out_specs=[pl.BlockSpec(memory_space=pltpu.VMEM)] * 2,
+        out_specs=pl.BlockSpec(memory_space=pltpu.VMEM),
         scratch_shapes=[
             vmem((4, BLK, auxw, occ), jnp.bfloat16),
             vmem((8, BLK, 128), jnp.bfloat16),
@@ -320,7 +318,6 @@
         ),
         cost_estimate=pl.CostEstimate(flops=2 * 2048 * cols * width, bytes_accessed=2 << 20, transcendentals=0),
     )(pltpu.with_memory_space_constraint(half_three, pltpu.HBM), pltpu.with_memory_space_constraint(block_mask.transpose(1, 2, 0), pltpu.HBM), pltpu.with_memory_space_constraint(panel_blocks, pltpu.HBM))
-    return mine + came
 
 
 def solution(mesh):

time: 67.4 us -> 67.4 us (level)
  the two profiles are of different devices: /device:TPU:16 before, /device:TPU:2 now
where the time goes in v6:
time: 67.4 us; the launch traced here: 67.3 us
  Pallas kernels  66.6 us (99%)
  local copies, waits for them, and re-layouts  0.71 us (1%)
    pallas_call x1, Pallas kernels, body(): pl.pallas_call(kernel, out_shape=jax.ShapeDtypeStruct((BLK, cols), jnp.fl...  66.6 us

profile of v6, /device:TPU:2, one launch (start us, length us, event | category | flops | bytes accessed | tf_op | source)
XLA Modules:
  0.0 67.3 jit_solution(880448853213659104)
XLA Ops:
  0.0 66.6 %shard_map.37 = f32[128,512]{1,0:T(8,128)S(1)} custom-call(bf16[512,4,256]{2,1,0:T(4,128)(2,1)} %half.1, s32[1,2,4]{2,1,0:T(2,128)} %bitcast.1, s32[16]{0:T(128)} %blocks_in.1), custom_call_target="tpu_custom_call" | custom-call | flops 2147483648 | bytes 2097152 | tf_op jit(solution)/shard_map/pallas_call | solution.py:284
  66.6 0.7 %copy.5 = f32[128,512]{1,0:T(8,128)} copy(f32[128,512]{1,0:T(8,128)S(1)} %shard_map.37) | data formatting | bytes 524288
